TPU v7x, 32 devices: a whole 2x2x4 slice. The times are simulated.
32 devices in a mesh: node: 8 (over y, x, core), head: 4 (over z).
Axes of the slice: x: 2, y: 2, z: 4, core: 2. Of those that a mesh axis runs over, the one named last changes fastest.
Arguments:
- features: bfloat16 [32768, 768], P(('node', 'head'))
- w_query: bfloat16 [768, 768], replicated
- w_key: bfloat16 [768, 768], replicated
- w_value: bfloat16 [768, 768], replicated, may hold values from -0.86328125 to 0.86328125
- w_out: bfloat16 [768, 768], replicated, may hold values from -0.21875 to 0.21875
- w_up: bfloat16 [768, 1536], replicated, may hold values from -0.21875 to 0.21875
- w_down: bfloat16 [1536, 768], replicated, may hold values from -0.21875 to 0.21875
- gain_attn: float32 [768], replicated, may hold values from 0.25 to 1.75
- gain_ffn: float32 [768], replicated, may hold values from 0.25 to 1.75
- send_list: int32 [8, 8, 16], P('node'), may hold values from 0 to 63
- edge_owner: int32 [512, 8], P('node'), may hold values from 0 to 7
- edge_slot: int32 [512, 8], P('node'), may hold values from 0 to 15
- edge_count: int32 [512], P('node'), may hold values from 1 to 8, as said below
Outputs:
- layer_out: bfloat16 [32768, 768], P(('node', 'head'))
Inputs may be any that keep to these rules, and one draw needn't show every extreme that they name: `edge_count`: at least one query block uses 1 entry; every query block of every fourth node group (0, 4, 8, ...) uses all 8.
All inputs are finite; a program needn't handle non-finite values.
Results may differ from a plain program's by a relative error of at most 0.0076.
Values may be sent and summed in bfloat16 or wider, within the bound.
A program may use at most 128 MiB of HBM per device.

v0:
```python
import math

import jax
import jax.numpy as jnp
from jax import lax
from jax.sharding import PartitionSpec as P

HDIM = 64
BLOCK = 64
MAXK = 8
CAP = 16


def normed(values, gain):
    center = values - jnp.mean(values, axis=-1, keepdims=True)
    spread = jnp.mean(center * center, axis=-1, keepdims=True)
    return center * lax.rsqrt(spread + 1e-05) * gain


def per_device(
    features,
    w_query,
    w_key,
    w_value,
    w_out,
    w_up,
    w_down,
    gain_attn,
    gain_ffn,
    send_list,
    edge_owner,
    edge_slot,
    edge_count,
):
    head_devs = lax.axis_size("head")
    head_index = lax.axis_index("head")
    local_rows, width = features.shape
    head_groups = math.gcd(width // HDIM, head_devs)
    node_parts = head_devs // head_groups
    part_index = head_index // head_groups
    head_cols = width // head_groups
    heads_here = head_cols // HDIM
    part_rows = local_rows // node_parts
    stacked = jnp.stack(
        [matrix.reshape(width, head_groups, head_cols) for matrix in (w_query, w_key, w_value)],
        axis=2,
    )
    w_all = stacked.reshape(width, 3 * width)
    made = jnp.dot(features, w_all, preferred_element_type=jnp.float32).astype(jnp.bfloat16)
    made = made.reshape(local_rows, head_groups, 3 * head_cols)
    made = jnp.tile(made, (1, node_parts, 1))
    moved = lax.all_to_all(made, "head", split_axis=1, concat_axis=0, tiled=True)
    projected = moved.reshape(local_rows * head_devs, 3 * head_cols)
    group_rows = projected.shape[0]
    blocks_here = group_rows // BLOCK
    pair_blocks = projected[:, head_cols:].reshape(blocks_here, BLOCK, 2 * head_cols)
    outgoing = jnp.take(pair_blocks, send_list.reshape(-1), axis=0)
    outgoing = outgoing.reshape(send_list.shape[1], send_list.shape[2], BLOCK, 2 * head_cols)
    incoming = lax.all_to_all(outgoing, "node", split_axis=0, concat_axis=0, tiled=True)
    incoming_flat = incoming.reshape(-1, BLOCK, 2 * head_cols)

    def select_part(array):
        rest = array.shape[1:]
        shaped = array.reshape((head_devs, node_parts, -1) + rest)
        picked = lax.dynamic_index_in_dim(shaped, part_index, 1, keepdims=False)
        return picked.reshape((-1,) + rest)

    query_blocks = select_part(projected[:, :head_cols].reshape(blocks_here, BLOCK, head_cols))
    own_blocks = select_part(pair_blocks)
    owner_part = select_part(edge_owner)
    slot_part = select_part(edge_slot)
    count_part = select_part(edge_count)
    my_blocks = query_blocks.shape[0]
    group_size = math.gcd(8, my_blocks)
    steps_count = my_blocks // group_size
    query_groups = query_blocks.reshape(steps_count, group_size, BLOCK, heads_here, HDIM)
    slot_ids = (owner_part * CAP + slot_part).reshape(steps_count, group_size, MAXK)
    count_groups = count_part.reshape(steps_count, group_size)
    own_groups = own_blocks.reshape(steps_count, group_size, BLOCK, 2 * head_cols)
    list_ids = jnp.arange(MAXK, dtype=jnp.int32)

    def attend(args):
        query_rows, slot_rows, count_rows, own_rows = args
        remote = jnp.take(incoming_flat, slot_rows.reshape(-1), axis=0)
        remote = remote.reshape(group_size, MAXK * BLOCK, 2 * head_cols)
        remote_keys = remote[:, :, :head_cols].reshape(group_size, -1, heads_here, HDIM)
        remote_values = remote[:, :, head_cols:].reshape(group_size, -1, heads_here, HDIM)
        own_keys = own_rows[:, :, :head_cols].reshape(group_size, BLOCK, heads_here, HDIM)
        own_values = own_rows[:, :, head_cols:].reshape(group_size, BLOCK, heads_here, HDIM)
        own_scores = jnp.einsum(
            "gqhd,gkhd->ghqk", query_rows, own_keys, preferred_element_type=jnp.float32
        ) / math.sqrt(HDIM)
        far_scores = jnp.einsum(
            "gqhd,gkhd->ghqk", query_rows, remote_keys, preferred_element_type=jnp.float32
        ) / math.sqrt(HDIM)
        valid = list_ids[None, :] < count_rows[:, None]
        valid = jnp.repeat(valid, BLOCK, axis=1)
        far_scores = jnp.where(valid[:, None, None, :], far_scores, -1e30)
        top = jnp.maximum(
            jnp.max(own_scores, axis=-1, keepdims=True), jnp.max(far_scores, axis=-1, keepdims=True)
        )
        own_weights = jnp.exp(own_scores - top)
        far_weights = jnp.exp(far_scores - top)
        total = jnp.sum(own_weights, axis=-1, keepdims=True) + jnp.sum(
            far_weights, axis=-1, keepdims=True
        )
        own_probs = (own_weights / total).astype(jnp.bfloat16)
        far_probs = (far_weights / total).astype(jnp.bfloat16)
        result = jnp.einsum(
            "ghqk,gkhd->gqhd", own_probs, own_values, preferred_element_type=jnp.float32
        )
        result = result + jnp.einsum(
            "ghqk,gkhd->gqhd", far_probs, remote_values, preferred_element_type=jnp.float32
        )
        return result.astype(jnp.bfloat16).reshape(group_size * BLOCK, head_cols)

    attended = lax.map(attend, (query_groups, slot_ids, count_groups, own_groups)).reshape(
        my_blocks * BLOCK, head_cols
    )
    spread_out = attended.reshape(head_devs, part_rows, head_cols)
    back = lax.all_to_all(spread_out, "head", split_axis=0, concat_axis=0, tiled=True)
    back = back.reshape(node_parts, head_groups, part_rows, head_cols)
    w_split = w_out.reshape(head_groups, head_cols, width)
    mixed = jnp.einsum("pgrc,gcd->prd", back, w_split, preferred_element_type=jnp.float32).reshape(
        local_rows, width
    )
    first = normed(features.astype(jnp.float32) + mixed, gain_attn).astype(jnp.bfloat16)
    hidden = jnp.maximum(jnp.dot(first, w_up, preferred_element_type=jnp.float32), 0.0).astype(
        jnp.bfloat16
    )
    total = first.astype(jnp.float32) + jnp.dot(hidden, w_down, preferred_element_type=jnp.float32)
    return normed(total, gain_ffn).astype(jnp.bfloat16)


def solution(mesh):
    return jax.shard_map(
        per_device,
        mesh=mesh,
        in_specs=(
            P(("node", "head"), None),
            P(),
            P(),
            P(),
            P(),
            P(),
            P(),
            P(),
            P(),
            P("node", None, None),
            P("node", None),
            P("node", None),
            P("node"),
        ),
        out_specs=P(("node", "head"), None),
        check_vma=False,
    )
```

profile of v0, /device:TPU:24, one launch (start us, length us, event | category | flops | bytes accessed | tf_op | source)
XLA Modules:
  0.0 546.5 jit_solution(564090081299456982)
XLA Ops:
  9.7 5.8 %convolution_convert_fusion = bf16[2304,1024]{1,0:T(8,128)(2,1)} fusion(bf16[768,2304]{0,1:T(8,128)(2,1)S(1)} %bitcast.120, bf16[1024,768]{1,0:T(8,128)(2,1)S(1)} %copy-done.6), kind=kOutput, calls=%fused_computation.38 | convolution fusion | flops 3626237952 | bytes 9830400 | tf_op jit(solution)/shard_map/dot_general | solution.py:49
  15.5 5.2 all-to-all-start
  20.9 102.3 %all-to-all-done = bf16[1024,4,576]{0,2,1:T(8,128)(2,1)} async-done(((bf16[1024,4,576]{0,2,1:T(8,128)(2,1)}), bf16[1024,4,576]{0,2,1:T(8,128)(2,1)}, u32[]{:S(2)}, u32[]{:S(2)}) %all-to-all-start) | async-done | bytes 4718624 | tf_op jit(solution)/shard_map/all_to_all | solution.py:52
  123.2 6.0 %copy.64 = bf16[4,1024,1,576]{1,0,3,2:T(4,128)(2,1)S(1)} copy(bf16[4,1024,1,576]{1,3,0,2:T(8,128)(2,1)} %bitcast.7) | data formatting | bytes 9437184 | tf_op jit(solution)/shard_map/all_to_all | solution.py:52
  136.2 4.7 copy.65
  140.8 6.0 %gather_fusion.1 = bf16[128,64,384]{2,1,0:T(8,128)(2,1)} fusion(bf16[64,64,384]{2,1,0:T(8,128)(2,1)} %bitcast.107, s32[1024]{0:T(1024)S(1)} %pad_clamp_fusion.1), kind=kCustom, calls=%fused_computation.1 | custom fusion | bytes 12583424 | tf_op jit(solution)/shard_map/jit(_take)/gather | solution.py:57
  146.8 6.2 %broadcast_select_fusion.1 = bf16[8,16,64,384]{3,2,1,0:T(8,128)(2,1)} fusion(bf16[8,16,64,384]{3,2,1,0:T(8,128)(2,1)} %bitcast.111, pred[8,16]{1,0:T(8,128)(4,1)S(1)} %compare_and_fusion.1), kind=kLoop, calls=%fused_computation.37 | loop fusion | flops 3145728 | bytes 12583040 | tf_op jit(solution)/shard_map/jit(_take)/select_n | solution.py:57
  153.0 5.1 all-to-all-start.1
  162.2 5.5 %reshape_reshape.15 = bf16[8,8,64,3,64]{2,1,0,4,3:T(8,128)(2,1)} reshape(bf16[4096,192]{0,1:T(8,128)(2,1)} %slice.33) | data formatting | bytes 3145728 | tf_op jit(solution)/shard_map/reshape;reshape | solution.py:76
  167.7 61.8 %all-to-all-done.1 = bf16[8,16,64,384]{3,2,1,0:T(8,128)(2,1)} async-done(((bf16[8,16,64,384]{3,2,1,0:T(8,128)(2,1)}), bf16[8,16,64,384]{3,2,1,0:T(8,128)(2,1)}, u32[]{:S(2)}, u32[]{:S(2)}) %all-to-all-start.1) | async-done | bytes 6291488 | tf_op jit(solution)/shard_map/all_to_all | solution.py:59
  229.5 244.8 %while.11 = (s32[]{:T(128)}, bf16[8,512,192]{1,2,0:T(8,128)(2,1)}, bf16[8,8,64,384]{3,2,1,0:T(8,128)(2,1)}, bf16[8,8,64,3,64]{2,1,0,4,3:T(8,128)(2,1)}, s32[8,8]...) while((s32[]{:T(128)}, bf16[8,512,192]{1,2,0:T(8,128)(2,1)}, ...), condition=%wide.region_5.6_spmd.clone, body=%wide.region_0.5_spmd.clone.sunk | while | flops 238385792 | bytes 64076852 | solution.py:117
  230.3 5.5 gather_fusion
  235.7 4.7 copy.82
  247.0 3.7 fusion.55
  260.9 5.5 gather_fusion
  266.3 4.7 copy.82
  291.5 5.5 gather_fusion
  296.9 4.7 copy.82
  322.1 5.5 gather_fusion
  327.5 4.7 copy.82
  352.7 5.5 gather_fusion
  358.1 4.7 copy.82
  383.3 5.5 gather_fusion
  388.7 4.7 copy.82
  413.9 5.5 gather_fusion
  419.4 4.7 copy.82
  444.5 5.5 gather_fusion
  449.9 4.7 copy.82
  477.7 3.7 reshape_reshape.17
  484.5 6.9 %all-to-all-start.2 = ((bf16[4,1024,192]{1,2,0:T(8,128)(2,1)}), bf16[4,1024,192]{1,2,0:T(8,128)(2,1)}, u32[]{:S(2)}, u32[]{:S(2)}) async-start(bf16[4,1024,192]{1,2,0:T(8,128)(2,1)} %copy.71), calls=%async_computation.2 | async-start | bytes 3145728 | tf_op jit(solution)/shard_map/all_to_all | solution.py:121
  494.0 29.3 %all-to-all-done.2 = bf16[4,1024,192]{1,2,0:T(8,128)(2,1)} async-done(((bf16[4,1024,192]{1,2,0:T(8,128)(2,1)}), bf16[4,1024,192]{1,2,0:T(8,128)(2,1)}, u32[]{:S(2)}, u32[]{:S(2)}) %all-to-all-start.2) | async-done | bytes 1572896 | tf_op jit(solution)/shard_map/all_to_all | solution.py:121
  528.8 10.8 %fusion.23 = (f32[1024]{0:T(1024)S(1)}, f32[1024,768]{0,1:T(8,128)}) fusion(bf16[1536,768]{1,0:T(8,128)(2,1)S(1)} %copy-done, bf16[768,1536]{1,0:T(8,128)(2,1)} %param.20, f32[1024,768]{0,1:T(8,128)} %copy-done.5, f32[768]{0:T(1024)S(1)} %copy-done.15, f32[1024]{0:T(1024)S(1)} %add_rsqrt_fusion.1, f32[1024]{0:T(1024)S(1)} %broadcast_multiply_fusion.1), kind=kOutput, calls=%fused_computation.61 | convolution fusion | flops 4843633664 | bytes 11025408 | tf_op jit(solution)/shard_map/dot_general | solution.py:131
  (339 shorter events, 201.4 us)
Async XLA Ops:
  0.0 528.8 %copy-start = (bf16[1536,768]{1,0:T(8,128)(2,1)S(1)}, bf16[1536,768]{1,0:T(8,128)(2,1)}, u32[]{:S(2)}) copy-start(bf16[1536,768]{1,0:T(8,128)(2,1)} %param.21) | copy-start | bytes 7077892
  15.5 5.3 copy-start.9
  15.5 107.7 %all-to-all-start = ((bf16[1024,4,576]{0,2,1:T(8,128)(2,1)}), bf16[1024,4,576]{0,2,1:T(8,128)(2,1)}, u32[]{:S(2)}, u32[]{:S(2)}) async-start(bf16[1024,4,576]{0,2,1:T(8,128)(2,1)} %bitcast.119), calls=%async_computation | async-start | bytes 9437184 | tf_op jit(solution)/shard_map/all_to_all | solution.py:52
  132.2 2.1 copy-start.3
  153.0 5.1 copy-start.10
  153.0 5.1 copy-start.11
  153.0 5.9 %copy-start.13 = (s32[64]{0:T(128)S(1)}, s32[64]{0:T(128)}, u32[]{:S(2)}) copy-start(s32[64]{0:T(128)} %param.27) | copy-start | bytes 772
  153.0 76.5 %all-to-all-start.1 = ((bf16[8,16,64,384]{3,2,1,0:T(8,128)(2,1)}), bf16[8,16,64,384]{3,2,1,0:T(8,128)(2,1)}, u32[]{:S(2)}, u32[]{:S(2)}) async-start(bf16[8,16,64,384]{3,2,1,0:T(8,128)(2,1)} %broadcast_select_fusion.1), calls=%async_computation.1 | async-start | bytes 12582912 | tf_op jit(solution)/shard_map/all_to_all | solution.py:59
  245.6 5.0 copy-start.7
  253.8 1.9 copy-start.1
  253.9 3.0 copy-start.2
  276.2 5.0 copy-start.7
  284.4 1.9 copy-start.1
  284.5 3.0 copy-start.2
  306.8 5.0 copy-start.7
  315.0 1.9 copy-start.1
  315.1 3.0 copy-start.2
  337.4 5.0 copy-start.7
  345.7 3.0 copy-start.2
  368.0 5.0 copy-start.7
  376.3 3.0 copy-start.2
  398.6 5.0 copy-start.7
  406.9 3.0 copy-start.2
  429.2 5.0 copy-start.7
  437.5 3.0 copy-start.2
  459.8 5.0 copy-start.7
  468.1 3.0 copy-start.2
  484.5 38.8 %copy-start.14 = (bf16[768,768]{1,0:T(8,128)(2,1)S(1)}, bf16[768,768]{1,0:T(8,128)(2,1)}, u32[]{:S(2)}) copy-start(bf16[768,768]{1,0:T(8,128)(2,1)} %param.19) | copy-start | bytes 3538948
  484.5 38.8 %all-to-all-start.2 = ((bf16[4,1024,192]{1,2,0:T(8,128)(2,1)}), bf16[4,1024,192]{1,2,0:T(8,128)(2,1)}, u32[]{:S(2)}, u32[]{:S(2)}) async-start(bf16[4,1024,192]{1,2,0:T(8,128)(2,1)} %copy.71), calls=%async_computation.2 | async-start | bytes 3145728 | tf_op jit(solution)/shard_map/all_to_all | solution.py:121
  526.7 2.0 copy-start.15
  539.6 2.8 copy-start.4
  539.6 2.8 copy-start.12
  (15 other events, 27.6 us)
where the time goes:
time: 555 us; the launch traced here: 547 us
  local copies, waits for them, and re-layouts  221 us (40%)
  waiting for transfers between devices  193 us (35%)
  matrix products  68.2 us (12%)
  other arithmetic  45.7 us (8%)
  starting transfers between devices  17.3 us (3%)
    all_to_all x1, waiting for transfers between devices, per_device(): lax.all_to_all(made, 'head', split_axis=1, concat_axis=0, tiled=True)  102 us
    gather x16, local copies, waits for them, and re-layouts, attend(): remote = jnp.take(incoming_flat, slot_rows.reshape(-1), axis=0)  81.1 us
    all_to_all x1, waiting for transfers between devices, per_device(): lax.all_to_all(outgoing, 'node', split_axis=0, concat_axis=0, tiled=True)  61.8 us
    dynamic_slice x32, local copies, waits for them, and re-layouts, per_device(): lax.map(attend, (query_groups, slot_ids, count_groups, own_groups))  35.9 us
    dot_general x8, matrix products, attend(): jnp.einsum('gqhd,gkhd->ghqk', query_rows, remote_keys, preferred_element_...  29.3 us
    all_to_all x1, waiting for transfers between devices, per_device(): lax.all_to_all(spread_out, 'head', split_axis=0, concat_axis=0, tiled=True)  29.3 us
    select_n x16, other arithmetic, attend(): remote = jnp.take(incoming_flat, slot_rows.reshape(-1), axis=0)  17.7 us
    unnamed x29, local copies, waits for them, and re-layouts  17.4 us
  transfers between devices with their start and end apart: 3, of which 3 were waited for; matrix products, arithmetic and copies ran while one was open for 2% of the time, Pallas kernels for 0%

commit v1 on v0

v1 whole, which is shorter than its diff:
```python
import functools
import math

import jax
import jax.numpy as jnp
from jax import lax
from jax.experimental import pallas as pl
from jax.experimental.pallas import tpu as pltpu
from jax.sharding import PartitionSpec as P

HDIM = 64
BLOCK = 64
MAXK = 8
CAP = 16
PAIR = 2 * HDIM
CHUNKS = (3,)
VMEM_LIMIT = 56 * 1024 * 1024


def vmem(count):
    return [pl.BlockSpec(memory_space=pltpu.VMEM)] * count


def smem(count):
    return [pl.BlockSpec(memory_space=pltpu.SMEM)] * count


def params():
    return pltpu.CompilerParams(vmem_limit_bytes=VMEM_LIMIT)


def normed(values, gain):
    center = values - jnp.mean(values, axis=-1, keepdims=True)
    spread = jnp.mean(center * center, axis=-1, keepdims=True)
    return center * lax.rsqrt(spread + 1e-05) * gain


def dot(a, b):
    return jnp.dot(a, b, preferred_element_type=jnp.float32)


def project_kv_kernel(head_groups, chunks, f_ref, wk_ref, wv_ref, *outs):
    rows = f_ref.shape[0]
    tile = min(rows, 256)
    heads = wk_ref.shape[1] // HDIM
    per_group = heads // head_groups
    for start in range(0, rows, tile):
        part = f_ref[start : start + tile, :]
        keys = dot(part, wk_ref[...]).astype(jnp.bfloat16)
        values = dot(part, wv_ref[...]).astype(jnp.bfloat16)
        for group in range(head_groups):
            head = group * per_group
            for size, out in zip(chunks, outs):
                for place in range(size):
                    cols = slice(head * HDIM, (head + 1) * HDIM)
                    both = jnp.concatenate([keys[:, cols], values[:, cols]], axis=1)
                    out[group, start : start + tile, place * PAIR : (place + 1) * PAIR] = both
                    head += 1


def project_q_kernel(head_groups, node_parts, f_ref, wq_ref, out):
    rows = f_ref.shape[0]
    half = rows // node_parts // 2
    group_cols = wq_ref.shape[1] // head_groups
    for part in range(node_parts):
        low = part * 2 * half
        first = dot(f_ref[low : low + half, :], wq_ref[...]) * (1.0 / math.sqrt(HDIM))
        second = dot(f_ref[low + half : low + 2 * half, :], wq_ref[...]) * (1.0 / math.sqrt(HDIM))
        first, second = first.astype(jnp.bfloat16), second.astype(jnp.bfloat16)
        for group in range(head_groups):
            cols = slice(group * group_cols, (group + 1) * group_cols)
            out[part * head_groups + group] = jnp.concatenate([first[:, cols], second[:, cols]], axis=1)


def gather_kernel(list_ref, src_ref, out_ref, sem):
    @pl.loop(0, out_ref.shape[0])
    def _(i):
        pltpu.make_async_copy(src_ref.at[list_ref[i]], out_ref.at[i], sem).start()

    pltpu.make_async_copy(out_ref, out_ref, sem).wait()


def attend_kernel(node_parts, chunks, part_ref, slot_ref, count_ref, q_ref, *rest):
    parts_count = len(chunks)
    owns, fars, out_ref = rest[:parts_count], rest[parts_count : 2 * parts_count], rest[-1]
    sources, half, width = q_ref.shape
    half_blocks = half // BLOCK
    heads = width // (2 * HDIM)
    part = part_ref[0]
    column = lax.broadcasted_iota(jnp.int32, (1, (MAXK + 1) * BLOCK), 1)
    lane = lax.broadcasted_iota(jnp.int32, (1, PAIR), 1)
    low = lane < HDIM

    def one(index, step):
        source = index // half_blocks
        i = index % half_blocks
        row = pl.multiple_of(i * BLOCK, BLOCK)
        results = []
        for side in range(2):
            block = (source * node_parts + part) * (2 * half_blocks) + side * half_blocks + i
            slots = [slot_ref[block * MAXK + j] for j in range(MAXK)]
            bias = jnp.where(column < (count_ref[block] + 1) * BLOCK, 0.0, -1e30)
            head = 0
            for size, own, far in zip(chunks, owns, fars):
                for place in range(size):
                    unit = side * heads + head
                    cols = slice(place * PAIR, (place + 1) * PAIR)
                    pair = q_ref[source, pl.ds(row, BLOCK), unit // 2 * PAIR : (unit // 2 + 1) * PAIR]
                    if unit % 2:
                        pair = jnp.concatenate([pair[:, HDIM:], pair[:, :HDIM]], axis=1)
                    query = jnp.where(low, pair, jnp.zeros_like(pair))
                    both = jnp.concatenate(
                        [own[block, :, cols]] + [far[slot, :, cols] for slot in slots], axis=0
                    )
                    scores = lax.dot_general(
                        query, both, (((1,), (1,)), ((), ())), preferred_element_type=jnp.float32
                    )
                    scores = scores + bias
                    top = jnp.max(scores, axis=-1, keepdims=True)
                    weights = jnp.exp(scores - top)
                    total = jnp.sum(weights, axis=-1, keepdims=True)
                    result = dot(weights.astype(jnp.bfloat16), both) / total
                    results.append(result)
                    head += 1
        for j in range(heads):
            left = results[2 * j]
            left = jnp.concatenate([left[:, HDIM:], left[:, :HDIM]], axis=1)
            merged = jnp.where(low, left, results[2 * j + 1])
            out_ref[source, pl.ds(row, BLOCK), j * PAIR : (j + 1) * PAIR] = merged.astype(jnp.bfloat16)
        return step

    lax.fori_loop(0, sources * half_blocks, one, 0)


def finish_kernel(head_groups, f_ref, b_ref, wo_ref, wu_ref, wd_ref, ga_ref, gf_ref, out_ref):
    devices, half, width = b_ref.shape
    cols = width // 2
    tile = min(half, 256)
    for part in range(devices // head_groups):
        for side in range(2):
            for start in range(0, half, tile):
                low = (part * 2 + side) * half + start
                attended = jnp.concatenate(
                    [
                        b_ref[part * head_groups + group, start : start + tile, side * cols : (side + 1) * cols]
                        for group in range(head_groups)
                    ],
                    axis=1,
                )
                mixed = f_ref[low : low + tile, :].astype(jnp.float32) + dot(attended, wo_ref[...])
                first = normed(mixed, ga_ref[...]).astype(jnp.bfloat16)
                hidden = jnp.maximum(dot(first, wu_ref[...]), 0.0).astype(jnp.bfloat16)
                total = first.astype(jnp.float32) + dot(hidden, wd_ref[...])
                out_ref[low : low + tile, :] = normed(total, gf_ref[...]).astype(jnp.bfloat16)


def per_device(
    features,
    w_query,
    w_key,
    w_value,
    w_out,
    w_up,
    w_down,
    gain_attn,
    gain_ffn,
    send_list,
    edge_owner,
    edge_slot,
    edge_count,
):
    head_devs = lax.axis_size("head")
    head_index = lax.axis_index("head")
    local_rows, width = features.shape
    head_groups = math.gcd(width // HDIM, head_devs)
    node_parts = head_devs // head_groups
    part_index = head_index // head_groups
    head_cols = width // head_groups
    half = local_rows // node_parts // 2
    bf16 = jnp.bfloat16
    group_blocks = head_devs * local_rows // BLOCK
    listed = send_list.reshape(-1)

    kvs = pl.pallas_call(
        functools.partial(project_kv_kernel, head_groups, CHUNKS),
        out_shape=[jax.ShapeDtypeStruct((head_groups, local_rows, c * PAIR), bf16) for c in CHUNKS],
        in_specs=vmem(3),
        out_specs=vmem(len(CHUNKS)),
        compiler_params=params(),
        cost_estimate=pl.CostEstimate(
            flops=4 * local_rows * width * width, bytes_accessed=8 * local_rows * width, transcendentals=0
        ),
    )(features, w_key, w_value)
    queries = pl.pallas_call(
        functools.partial(project_q_kernel, head_groups, node_parts),
        out_shape=jax.ShapeDtypeStruct((head_devs, half, 2 * head_cols), bf16),
        in_specs=vmem(2),
        out_specs=vmem(1)[0],
        compiler_params=params(),
        cost_estimate=pl.CostEstimate(
            flops=2 * local_rows * width * width, bytes_accessed=6 * local_rows * width, transcendentals=0
        ),
    )(features, w_query)

    owns, fars = [], []
    for made in kvs:
        cols = made.shape[-1]
        made = jnp.tile(made, (node_parts, 1, 1))
        own = lax.all_to_all(made, "head", split_axis=0, concat_axis=0, tiled=True)
        own = own.reshape(group_blocks, BLOCK, cols)
        outgoing = pl.pallas_call(
            gather_kernel,
            out_shape=jax.ShapeDtypeStruct((listed.shape[0], BLOCK, cols), bf16),
            in_specs=smem(1) + [pl.BlockSpec(memory_space=pl.ANY)],
            out_specs=pl.BlockSpec(memory_space=pl.ANY),
            scratch_shapes=[pltpu.SemaphoreType.DMA],
        )(listed, own)
        far = lax.all_to_all(outgoing, "node", split_axis=0, concat_axis=0, tiled=True)
        owns.append(own)
        fars.append(far)
    queries = lax.all_to_all(queries, "head", split_axis=0, concat_axis=0, tiled=True)

    slots = (edge_owner * CAP + edge_slot).reshape(-1)
    attended = pl.pallas_call(
        functools.partial(attend_kernel, node_parts, CHUNKS),
        out_shape=jax.ShapeDtypeStruct((head_devs, half, 2 * head_cols), bf16),
        in_specs=smem(3) + vmem(1 + 2 * len(CHUNKS)),
        out_specs=vmem(1)[0],
        compiler_params=params(),
    )(part_index.astype(jnp.int32).reshape(1), slots, edge_count, queries, *owns, *fars)
    back = lax.all_to_all(attended, "head", split_axis=0, concat_axis=0, tiled=True)

    return pl.pallas_call(
        functools.partial(finish_kernel, head_groups),
        out_shape=jax.ShapeDtypeStruct((local_rows, width), bf16),
        in_specs=vmem(7),
        out_specs=vmem(1)[0],
        compiler_params=params(),
    )(features, back, w_out, w_up, w_down, gain_attn.reshape(1, -1), gain_ffn.reshape(1, -1))


def solution(mesh):
    return jax.shard_map(
        per_device,
        mesh=mesh,
        in_specs=(
            P(("node", "head"), None),
            P(),
            P(),
            P(),
            P(),
            P(),
            P(),
            P(),
            P(),
            P("node", None, None),
            P("node", None),
            P("node", None),
            P("node"),
        ),
        out_specs=P(("node", "head"), None),
        check_vma=False,
    )
```

time: 555 us -> 475 us (0.86)
  Pallas kernels: 0 us -> 279 us
  local copies, waits for them, and re-layouts: 221 us -> 3.76 us
  matrix products: 68.2 us -> 0 us
  other arithmetic: 45.7 us -> 0.01 us
  waiting for transfers between devices: 193 us -> 165 us
    pallas_call x0 -> x5, Pallas kernels: none -> 279 us  [the longest x1 192 us: per_device(): pl.pallas_call(gather_kernel, out_shape=jax.ShapeDtypeStruct((listed.shap...]
    gather x17 -> x0, local copies, waits for them, and re-layouts: 87.1 us -> none  [the longest x16 81.1 us: attend(): remote = jnp.take(incoming_flat, slot_rows.reshape(-1), axis=0)]
    dot_general x35 -> x0, matrix products: 68.2 us -> none  [the longest x8 29.3 us: attend(): jnp.einsum('gqhd,gkhd->ghqk', query_rows, remote_keys, preferred_element_...]
    all_to_all x2 -> x3, waiting for transfers between devices: 132 us -> 94.4 us  [the longest x1 64 us: per_device(): own = lax.all_to_all(made, 'head', split_axis=0, concat_axis=0, tiled=True)]
    dynamic_slice x32 -> x0, local copies, waits for them, and re-layouts: 35.9 us -> none  [per_device(): lax.map(attend, (query_groups, slot_ids, count_groups, own_groups))]
    slice x19 -> x0, local copies, waits for them, and re-layouts: 24.9 us -> none  [the longest x8 15.3 us: attend(): remote[:, :, :head_cols].reshape(group_size, -1, heads_here, HDIM)]
    select_n x18 -> x0, other arithmetic: 23.9 us -> none  [the longest x16 17.7 us: attend(): remote = jnp.take(incoming_flat, slot_rows.reshape(-1), axis=0)]
    unnamed x29 -> x14, local copies, waits for them, and re-layouts: 17.4 us -> 1.2 us
  transfers between devices with their start and end apart: 3 -> 4, of which waited for: 3 -> 3; matrix products, arithmetic and copies ran while one was open for 2% -> 1% of each run, Pallas kernels for 0% -> 42%
where the time goes in v1:
time: 475 us; the launch traced here: 470 us
  Pallas kernels  279 us (59%)
  waiting for transfers between devices  165 us (35%)
  starting transfers between devices  21.8 us (5%)
    pallas_call x1, Pallas kernels, per_device(): pl.pallas_call(gather_kernel, out_shape=jax.ShapeDtypeStruct((listed.shap...  192 us
    all_to_all x1, waiting for transfers between devices, per_device(): lax.all_to_all(outgoing, 'node', split_axis=0, concat_axis=0, tiled=True)  70.8 us
    all_to_all x1, waiting for transfers between devices, per_device(): own = lax.all_to_all(made, 'head', split_axis=0, concat_axis=0, tiled=True)  64 us
    pallas_call x1, Pallas kernels, per_device(): pl.pallas_call(functools.partial(attend_kernel, node_parts, CHUNKS), out_...  62.8 us
    all_to_all x1, waiting for transfers between devices, per_device(): lax.all_to_all(attended, 'head', split_axis=0, concat_axis=0, tiled=True)  30.4 us
    pallas_call x1, Pallas kernels, per_device(): pl.pallas_call(functools.partial(finish_kernel, head_groups), out_shape=j...  13.5 us
  transfers between devices with their start and end apart: 4, of which 3 were waited for; matrix products, arithmetic and copies ran while one was open for 1% of the time, Pallas kernels for 42%

profile of v1, /device:TPU:24, one launch (start us, length us, event | category | flops | bytes accessed | tf_op | source)
XLA Modules:
  0.0 470.3 jit_solution(6713453530960355584)
XLA Ops:
  0.0 6.4 %shard_map.128 = bf16[4,1024,384]{2,1,0:T(8,128)(2,1)} custom-call(bf16[1024,768]{1,0:T(8,128)(2,1)} %f_ref.5, bf16[768,768]{1,0:T(8,128)(2,1)} %wk_ref.1, bf16[768,768]{1,0:T(8,128)(2,1)} %wv_ref.1), custom_call_target="tpu_custom_call" | custom-call | flops 2415919104 | bytes 6291456 | tf_op jit(solution)/shard_map/pallas_call | solution.py:184
  6.4 5.1 %all-to-all-start.1 = ((bf16[4,1024,384]{2,1,0:T(8,128)(2,1)}), bf16[4,1024,384]{2,1,0:T(8,128)(2,1)S(1)}, u32[]{:S(2)}, u32[]{:S(2)}) async-start(bf16[4,1024,384]{2,1,0:T(8,128)(2,1)} %shard_map.128), calls=%async_computation.1 | async-start | bytes 6291456 | tf_op jit(solution)/shard_map/all_to_all | solution.py:209
  11.5 4.3 shard_map.127
  15.9 0.0 copy-start.6
  15.9 64.0 %all-to-all-done.1 = bf16[4,1024,384]{2,1,0:T(8,128)(2,1)S(1)} async-done(((bf16[4,1024,384]{2,1,0:T(8,128)(2,1)}), bf16[4,1024,384]{2,1,0:T(8,128)(2,1)S(1)}, u32[]{:S(2)}, u32[]{:S(2)}) %all-to-all-start.1) | async-done | bytes 3145760 | tf_op jit(solution)/shard_map/all_to_all | solution.py:209
  79.8 0.0 copy-start
  79.8 6.7 %all-to-all-start = ((bf16[4,512,384]{2,1,0:T(8,128)(2,1)}), bf16[4,512,384]{2,1,0:T(8,128)(2,1)}, u32[]{:S(2)}, u32[]{:S(2)}) async-start(bf16[4,512,384]{2,1,0:T(8,128)(2,1)} %shard_map.127), calls=%async_computation | async-start | bytes 3145728 | tf_op jit(solution)/shard_map/all_to_all | solution.py:221
  86.5 0.0 copy-done.6
  86.5 0.6 reshape.21.list_ref
  87.1 0.0 copy-done
  87.1 192.4 %shard_map.129 = bf16[128,64,384]{2,1,0:T(8,128)(2,1)} custom-call(s32[128]{0:T(128)} %reshape.21.list_ref, bf16[64,64,384]{2,1,0:T(8,128)(2,1)} %bitcast.2), custom_call_target="tpu_custom_call" | custom-call | tf_op jit(solution)/shard_map/pallas_call | solution.py:211
  279.5 0.0 copy-start.2
  279.5 0.0 copy-start.3
  279.5 0.0 all-to-all-done.q_ref
  279.5 4.8 %all-to-all-start.2 = ((bf16[128,64,384]{2,1,0:T(8,128)(2,1)}), bf16[128,64,384]{2,1,0:T(8,128)(2,1)}, u32[]{:S(2)}, u32[]{:S(2)}) async-start(bf16[128,64,384]{2,1,0:T(8,128)(2,1)} %shard_map.129), calls=%async_computation.2 | async-start | bytes 12582912 | tf_op jit(solution)/shard_map/all_to_all | solution.py:218
  284.3 0.0 copy-done.2
  284.3 0.0 copy-done.3
  284.4 0.1 copy.14
  284.5 0.7 reshape.19.slot_ref
  285.1 70.8 %all-to-all-done.2.rest_1_ = bf16[128,64,384]{2,1,0:T(8,128)(2,1)} async-done(((bf16[128,64,384]{2,1,0:T(8,128)(2,1)}), bf16[128,64,384]{2,1,0:T(8,128)(2,1)}, u32[]{:S(2)}, u32[]{:S(2)}) %all-to-all-start.2) | async-done | bytes 6291488 | tf_op jit(solution)/shard_map/all_to_all | solution.py:218
  355.9 62.8 %shard_map.130 = bf16[4,512,384]{2,1,0:T(8,128)(2,1)} custom-call(s32[1]{0:T(128)} %bitcast.part_ref, s32[512]{0:T(512)} %reshape.19.slot_ref, s32[64]{0:T(128)} %count_ref.1, bf16[4,512,384]{2,1,0:T(8,128)(2,1)} %all-to-all-done.q_ref, bf16[64,64,384]{2,1,0:T(8,128)(2,1)} %bitcast.3, bf16[128,64,384]{2,1,0:T(8,128)(2,1)} %all-to-all-done.2.rest_1_), custom_call_target="tpu_custom_call" | custom-call | tf_op jit(solution)/shard_map/pallas_call | solution.py:224
  418.8 0.0 copy-start.4
  418.8 0.0 copy-start.5
  418.8 5.2 %all-to-all-start.3 = ((bf16[4,512,384]{2,1,0:T(8,128)(2,1)}), bf16[4,512,384]{2,1,0:T(8,128)(2,1)S(1)}, u32[]{:S(2)}, u32[]{:S(2)}) async-start(bf16[4,512,384]{2,1,0:T(8,128)(2,1)} %shard_map.130), calls=%async_computation.3 | async-start | bytes 3145728 | tf_op jit(solution)/shard_map/all_to_all | solution.py:231
  424.0 0.0 copy-done.4
  424.0 0.6 reshape.22.ga_ref
  424.6 0.0 copy-done.5
  424.6 0.6 reshape.23.gf_ref
  425.2 30.4 %all-to-all-done.3.b_ref = bf16[4,512,384]{2,1,0:T(8,128)(2,1)S(1)} async-done(((bf16[4,512,384]{2,1,0:T(8,128)(2,1)}), bf16[4,512,384]{2,1,0:T(8,128)(2,1)S(1)}, u32[]{:S(2)}, u32[]{:S(2)}) %all-to-all-start.3) | async-done | bytes 1572896 | tf_op jit(solution)/shard_map/all_to_all | solution.py:231
  455.6 0.0 copy-start.1
  455.6 1.2 copy-done.1
  456.8 13.5 %shard_map.131 = bf16[1024,768]{1,0:T(8,128)(2,1)} custom-call(bf16[1024,768]{1,0:T(8,128)(2,1)} %f_ref.5, bf16[4,512,384]{2,1,0:T(8,128)(2,1)} %copy-done.1, bf16[768,768]{1,0:T(8,128)(2,1)} %wo_ref.1, bf16[768,1536]{1,0:T(8,128)(2,1)} %wu_ref.1, bf16[1536,768]{1,0:T(8,128)(2,1)} %wd_ref.1, f32[1,768]{1,0:T(1,128)} %reshape.22.ga_ref, f32[1,768]{1,0:T(1,128)} %reshape.23.gf_ref), custom_call_target="tpu_custom_call" | custom-call | tf_op jit(solution)/shard_map/pallas_call | solution.py:233
  (1 shorter events, 0.0 us)
Async XLA Ops:
  6.4 73.4 %all-to-all-start.1 = ((bf16[4,1024,384]{2,1,0:T(8,128)(2,1)}), bf16[4,1024,384]{2,1,0:T(8,128)(2,1)S(1)}, u32[]{:S(2)}, u32[]{:S(2)}) async-start(bf16[4,1024,384]{2,1,0:T(8,128)(2,1)} %shard_map.128), calls=%async_computation.1 | async-start | bytes 6291456 | tf_op jit(solution)/shard_map/all_to_all | solution.py:209
  15.9 70.6 %copy-start.6 = (s32[1,8,16]{2,1,0:T(8,128)S(1)}, s32[1,8,16]{2,1,0:T(8,128)}, u32[]{:S(2)}) copy-start(s32[1,8,16]{2,1,0:T(8,128)} %param.22) | copy-start | bytes 1540
  79.8 7.3 %copy-start = (bf16[4,1024,384]{2,1,0:T(8,128)(2,1)}, bf16[4,1024,384]{2,1,0:T(8,128)(2,1)S(1)}, u32[]{:S(2)}) copy-start(bf16[4,1024,384]{2,1,0:T(8,128)(2,1)S(1)} %all-to-all-done.1) | copy-start | bytes 9437188
  79.8 199.7 %all-to-all-start = ((bf16[4,512,384]{2,1,0:T(8,128)(2,1)}), bf16[4,512,384]{2,1,0:T(8,128)(2,1)}, u32[]{:S(2)}, u32[]{:S(2)}) async-start(bf16[4,512,384]{2,1,0:T(8,128)(2,1)} %shard_map.127), calls=%async_computation | async-start | bytes 3145728 | tf_op jit(solution)/shard_map/all_to_all | solution.py:221
  279.5 4.8 %copy-start.2 = (s32[64,8]{0,1:T(8,128)S(1)}, s32[64,8]{0,1:T(8,128)}, u32[]{:S(2)}) copy-start(s32[64,8]{0,1:T(8,128)} %param.24) | copy-start | bytes 6148
  279.5 4.8 %copy-start.3 = (s32[64,8]{0,1:T(8,128)S(1)}, s32[64,8]{0,1:T(8,128)}, u32[]{:S(2)}) copy-start(s32[64,8]{0,1:T(8,128)} %param.23) | copy-start | bytes 6148
  279.5 76.4 %all-to-all-start.2 = ((bf16[128,64,384]{2,1,0:T(8,128)(2,1)}), bf16[128,64,384]{2,1,0:T(8,128)(2,1)}, u32[]{:S(2)}, u32[]{:S(2)}) async-start(bf16[128,64,384]{2,1,0:T(8,128)(2,1)} %shard_map.129), calls=%async_computation.2 | async-start | bytes 12582912 | tf_op jit(solution)/shard_map/all_to_all | solution.py:218
  418.8 5.2 %copy-start.4 = (f32[768]{0:T(1024)S(1)}, f32[768]{0:T(1024)}, u32[]{:S(2)}) copy-start(f32[768]{0:T(1024)} %param.20) | copy-start | bytes 9220
  418.8 5.8 %copy-start.5 = (f32[768]{0:T(1024)S(1)}, f32[768]{0:T(1024)}, u32[]{:S(2)}) copy-start(f32[768]{0:T(1024)} %param.21) | copy-start | bytes 9220
  418.8 36.9 %all-to-all-start.3 = ((bf16[4,512,384]{2,1,0:T(8,128)(2,1)}), bf16[4,512,384]{2,1,0:T(8,128)(2,1)S(1)}, u32[]{:S(2)}, u32[]{:S(2)}) async-start(bf16[4,512,384]{2,1,0:T(8,128)(2,1)} %shard_map.130), calls=%async_computation.3 | async-start | bytes 3145728 | tf_op jit(solution)/shard_map/all_to_all | solution.py:231
  455.6 1.2 copy-start.1

commit v2 on v1

--- a/solution.py
+++ b/solution.py
@@ -72,12 +72,12 @@
             out[part * head_groups + group] = jnp.concatenate([first[:, cols], second[:, cols]], axis=1)
 
 
-def gather_kernel(list_ref, src_ref, out_ref, sem):
-    @pl.loop(0, out_ref.shape[0])
-    def _(i):
-        pltpu.make_async_copy(src_ref.at[list_ref[i]], out_ref.at[i], sem).start()
-
-    pltpu.make_async_copy(out_ref, out_ref, sem).wait()
+def gather_kernel(list_ref, src_ref, out_ref):
+    def one(i, step):
+        out_ref[i] = src_ref[list_ref[i]]
+        return step
+
+    lax.fori_loop(0, out_ref.shape[0], one, 0, unroll=4)
 
 
 def attend_kernel(node_parts, chunks, part_ref, slot_ref, count_ref, q_ref, *rest):
@@ -211,9 +211,9 @@
         outgoing = pl.pallas_call(
             gather_kernel,
             out_shape=jax.ShapeDtypeStruct((listed.shape[0], BLOCK, cols), bf16),
-            in_specs=smem(1) + [pl.BlockSpec(memory_space=pl.ANY)],
-            out_specs=pl.BlockSpec(memory_space=pl.ANY),
-            scratch_shapes=[pltpu.SemaphoreType.DMA],
+            in_specs=smem(1) + vmem(1),
+            out_specs=vmem(1)[0],
+            compiler_params=params(),
         )(listed, own)
         far = lax.all_to_all(outgoing, "node", split_axis=0, concat_axis=0, tiled=True)
         owns.append(own)

time: 475 us -> 317 us (0.67)
  Pallas kernels: 279 us -> 92.5 us
  waiting for transfers between devices: 165 us -> 194 us
    pallas_call x1, Pallas kernels: 192 us -> 5.37 us  [per_device(): pl.pallas_call(gather_kernel, out_shape=jax.ShapeDtypeStruct((listed.shap...]
    all_to_all x1, waiting for transfers between devices: 0.01 us -> 28.2 us  [per_device(): lax.all_to_all(queries, 'head', split_axis=0, concat_axis=0, tiled=True)]
  transfers between devices with their start and end apart: 4 -> 4, of which waited for: 3 -> 4; matrix products, arithmetic and copies ran while one was open for 1% -> 1% of each run, Pallas kernels for 42% -> 3%
where the time goes in v2:
time: 317 us; the launch traced here: 313 us
  waiting for transfers between devices  194 us (61%)
  Pallas kernels  92.5 us (29%)
  starting transfers between devices  22.6 us (7%)
  local copies, waits for them, and re-layouts  3.76 us (1%)
    all_to_all x1, waiting for transfers between devices, per_device(): lax.all_to_all(outgoing, 'node', split_axis=0, concat_axis=0, tiled=True)  70.8 us
    all_to_all x1, waiting for transfers between devices, per_device(): own = lax.all_to_all(made, 'head', split_axis=0, concat_axis=0, tiled=True)  64 us
    pallas_call x1, Pallas kernels, per_device(): pl.pallas_call(functools.partial(attend_kernel, node_parts, CHUNKS), out_...  62.8 us
    all_to_all x1, waiting for transfers between devices, per_device(): lax.all_to_all(attended, 'head', split_axis=0, concat_axis=0, tiled=True)  30.7 us
    all_to_all x1, waiting for transfers between devices, per_device(): lax.all_to_all(queries, 'head', split_axis=0, concat_axis=0, tiled=True)  28.2 us
    pallas_call x1, Pallas kernels, per_device(): pl.pallas_call(functools.partial(finish_kernel, head_groups), out_shape=j...  13.5 us
    all_to_all x1, starting transfers between devices, per_device(): lax.all_to_all(queries, 'head', split_axis=0, concat_axis=0, tiled=True)  6.68 us
    pallas_call x1, Pallas kernels, per_device(): pl.pallas_call(functools.partial(project_kv_kernel, head_groups, CHUNKS),...  6.42 us
  transfers between devices with their start and end apart: 4, of which 4 were waited for; matrix products, arithmetic and copies ran while one was open for 1% of the time, Pallas kernels for 3%

profile of v2, /device:TPU:24, one launch (start us, length us, event | category | flops | bytes accessed | tf_op | source)
XLA Modules:
  0.0 312.6 jit_solution(16228658316570114826)
XLA Ops:
  0.0 6.4 %shard_map.128 = bf16[4,1024,384]{2,1,0:T(8,128)(2,1)} custom-call(bf16[1024,768]{1,0:T(8,128)(2,1)} %f_ref.5, bf16[768,768]{1,0:T(8,128)(2,1)} %wk_ref.1, bf16[768,768]{1,0:T(8,128)(2,1)} %wv_ref.1), custom_call_target="tpu_custom_call" | custom-call | flops 2415919104 | bytes 6291456 | tf_op jit(solution)/shard_map/pallas_call | solution.py:184
  6.4 5.1 %all-to-all-start.1 = ((bf16[4,1024,384]{2,1,0:T(8,128)(2,1)}), bf16[4,1024,384]{2,1,0:T(8,128)(2,1)S(1)}, u32[]{:S(2)}, u32[]{:S(2)}) async-start(bf16[4,1024,384]{2,1,0:T(8,128)(2,1)} %shard_map.128), calls=%async_computation.1 | async-start | bytes 6291456 | tf_op jit(solution)/shard_map/all_to_all | solution.py:209
  11.5 4.3 %shard_map.127 = bf16[4,512,384]{2,1,0:T(8,128)(2,1)} custom-call(bf16[1024,768]{1,0:T(8,128)(2,1)} %f_ref.5, bf16[768,768]{1,0:T(8,128)(2,1)} %wq_ref.1), custom_call_target="tpu_custom_call" | custom-call | flops 1207959552 | bytes 4718592 | tf_op jit(solution)/shard_map/pallas_call | solution.py:194
  15.9 0.0 copy-start.6
  15.9 64.0 %all-to-all-done.1 = bf16[4,1024,384]{2,1,0:T(8,128)(2,1)S(1)} async-done(((bf16[4,1024,384]{2,1,0:T(8,128)(2,1)}), bf16[4,1024,384]{2,1,0:T(8,128)(2,1)S(1)}, u32[]{:S(2)}, u32[]{:S(2)}) %all-to-all-start.1) | async-done | bytes 3145760 | tf_op jit(solution)/shard_map/all_to_all | solution.py:209
  79.8 0.0 copy-start
  79.8 6.7 %all-to-all-start = ((bf16[4,512,384]{2,1,0:T(8,128)(2,1)}), bf16[4,512,384]{2,1,0:T(8,128)(2,1)}, u32[]{:S(2)}, u32[]{:S(2)}) async-start(bf16[4,512,384]{2,1,0:T(8,128)(2,1)} %shard_map.127), calls=%async_computation | async-start | bytes 3145728 | tf_op jit(solution)/shard_map/all_to_all | solution.py:221
  86.5 0.0 copy-done.6
  86.5 0.6 reshape.21.list_ref
  87.1 0.0 copy-done
  87.1 5.4 %shard_map.129 = bf16[128,64,384]{2,1,0:T(8,128)(2,1)} custom-call(s32[128]{0:T(128)} %reshape.21.list_ref, bf16[64,64,384]{2,1,0:T(8,128)(2,1)} %bitcast.2), custom_call_target="tpu_custom_call" | custom-call | tf_op jit(solution)/shard_map/pallas_call | solution.py:211
  92.5 0.0 copy-start.2
  92.5 0.0 copy-start.3
  92.5 28.2 %all-to-all-done.q_ref = bf16[4,512,384]{2,1,0:T(8,128)(2,1)} async-done(((bf16[4,512,384]{2,1,0:T(8,128)(2,1)}), bf16[4,512,384]{2,1,0:T(8,128)(2,1)}, u32[]{:S(2)}, u32[]{:S(2)}) %all-to-all-start) | async-done | bytes 1572896 | tf_op jit(solution)/shard_map/all_to_all | solution.py:221
  120.7 4.8 %all-to-all-start.2 = ((bf16[128,64,384]{2,1,0:T(8,128)(2,1)}), bf16[128,64,384]{2,1,0:T(8,128)(2,1)}, u32[]{:S(2)}, u32[]{:S(2)}) async-start(bf16[128,64,384]{2,1,0:T(8,128)(2,1)} %shard_map.129), calls=%async_computation.2 | async-start | bytes 12582912 | tf_op jit(solution)/shard_map/all_to_all | solution.py:218
  125.5 0.0 copy-done.2
  125.5 0.0 copy-done.3
  125.5 0.1 copy.14
  125.6 0.7 reshape.19.slot_ref
  126.3 70.8 %all-to-all-done.2.rest_1_ = bf16[128,64,384]{2,1,0:T(8,128)(2,1)} async-done(((bf16[128,64,384]{2,1,0:T(8,128)(2,1)}), bf16[128,64,384]{2,1,0:T(8,128)(2,1)}, u32[]{:S(2)}, u32[]{:S(2)}) %all-to-all-start.2) | async-done | bytes 6291488 | tf_op jit(solution)/shard_map/all_to_all | solution.py:218
  197.1 62.8 %shard_map.130 = bf16[4,512,384]{2,1,0:T(8,128)(2,1)} custom-call(s32[1]{0:T(128)} %bitcast.part_ref, s32[512]{0:T(512)} %reshape.19.slot_ref, s32[64]{0:T(128)} %count_ref.1, bf16[4,512,384]{2,1,0:T(8,128)(2,1)} %all-to-all-done.q_ref, bf16[64,64,384]{2,1,0:T(8,128)(2,1)} %bitcast.3, bf16[128,64,384]{2,1,0:T(8,128)(2,1)} %all-to-all-done.2.rest_1_), custom_call_target="tpu_custom_call" | custom-call | tf_op jit(solution)/shard_map/pallas_call | solution.py:224
  259.9 0.0 copy-start.4
  259.9 0.0 copy-start.5
  259.9 6.0 %all-to-all-start.3 = ((bf16[4,512,384]{2,1,0:T(8,128)(2,1)}), bf16[4,512,384]{2,1,0:T(8,128)(2,1)S(1)}, u32[]{:S(2)}, u32[]{:S(2)}) async-start(bf16[4,512,384]{2,1,0:T(8,128)(2,1)} %shard_map.130), calls=%async_computation.3 | async-start | bytes 3145728 | tf_op jit(solution)/shard_map/all_to_all | solution.py:231
  266.0 0.0 copy-done.4
  266.0 0.6 reshape.22.ga_ref
  266.6 0.0 copy-done.5
  266.6 0.6 reshape.23.gf_ref
  267.2 30.7 %all-to-all-done.3.b_ref = bf16[4,512,384]{2,1,0:T(8,128)(2,1)S(1)} async-done(((bf16[4,512,384]{2,1,0:T(8,128)(2,1)}), bf16[4,512,384]{2,1,0:T(8,128)(2,1)S(1)}, u32[]{:S(2)}, u32[]{:S(2)}) %all-to-all-start.3) | async-done | bytes 1572896 | tf_op jit(solution)/shard_map/all_to_all | solution.py:231
  297.9 0.0 copy-start.1
  297.9 1.2 copy-done.1
  299.0 13.5 %shard_map.131 = bf16[1024,768]{1,0:T(8,128)(2,1)} custom-call(bf16[1024,768]{1,0:T(8,128)(2,1)} %f_ref.5, bf16[4,512,384]{2,1,0:T(8,128)(2,1)} %copy-done.1, bf16[768,768]{1,0:T(8,128)(2,1)} %wo_ref.1, bf16[768,1536]{1,0:T(8,128)(2,1)} %wu_ref.1, bf16[1536,768]{1,0:T(8,128)(2,1)} %wd_ref.1, f32[1,768]{1,0:T(1,128)} %reshape.22.ga_ref, f32[1,768]{1,0:T(1,128)} %reshape.23.gf_ref), custom_call_target="tpu_custom_call" | custom-call | tf_op jit(solution)/shard_map/pallas_call | solution.py:233
  (1 shorter events, 0.0 us)
Async XLA Ops:
  6.4 73.4 %all-to-all-start.1 = ((bf16[4,1024,384]{2,1,0:T(8,128)(2,1)}), bf16[4,1024,384]{2,1,0:T(8,128)(2,1)S(1)}, u32[]{:S(2)}, u32[]{:S(2)}) async-start(bf16[4,1024,384]{2,1,0:T(8,128)(2,1)} %shard_map.128), calls=%async_computation.1 | async-start | bytes 6291456 | tf_op jit(solution)/shard_map/all_to_all | solution.py:209
  15.9 70.6 %copy-start.6 = (s32[1,8,16]{2,1,0:T(8,128)S(1)}, s32[1,8,16]{2,1,0:T(8,128)}, u32[]{:S(2)}) copy-start(s32[1,8,16]{2,1,0:T(8,128)} %param.22) | copy-start | bytes 1540
  79.8 7.3 %copy-start = (bf16[4,1024,384]{2,1,0:T(8,128)(2,1)}, bf16[4,1024,384]{2,1,0:T(8,128)(2,1)S(1)}, u32[]{:S(2)}) copy-start(bf16[4,1024,384]{2,1,0:T(8,128)(2,1)S(1)} %all-to-all-done.1) | copy-start | bytes 9437188
  79.8 40.9 %all-to-all-start = ((bf16[4,512,384]{2,1,0:T(8,128)(2,1)}), bf16[4,512,384]{2,1,0:T(8,128)(2,1)}, u32[]{:S(2)}, u32[]{:S(2)}) async-start(bf16[4,512,384]{2,1,0:T(8,128)(2,1)} %shard_map.127), calls=%async_computation | async-start | bytes 3145728 | tf_op jit(solution)/shard_map/all_to_all | solution.py:221
  92.5 33.0 %copy-start.2 = (s32[64,8]{0,1:T(8,128)S(1)}, s32[64,8]{0,1:T(8,128)}, u32[]{:S(2)}) copy-start(s32[64,8]{0,1:T(8,128)} %param.24) | copy-start | bytes 6148
  92.5 33.0 %copy-start.3 = (s32[64,8]{0,1:T(8,128)S(1)}, s32[64,8]{0,1:T(8,128)}, u32[]{:S(2)}) copy-start(s32[64,8]{0,1:T(8,128)} %param.23) | copy-start | bytes 6148
  120.7 76.4 %all-to-all-start.2 = ((bf16[128,64,384]{2,1,0:T(8,128)(2,1)}), bf16[128,64,384]{2,1,0:T(8,128)(2,1)}, u32[]{:S(2)}, u32[]{:S(2)}) async-start(bf16[128,64,384]{2,1,0:T(8,128)(2,1)} %shard_map.129), calls=%async_computation.2 | async-start | bytes 12582912 | tf_op jit(solution)/shard_map/all_to_all | solution.py:218
  259.9 6.0 %copy-start.4 = (f32[768]{0:T(1024)S(1)}, f32[768]{0:T(1024)}, u32[]{:S(2)}) copy-start(f32[768]{0:T(1024)} %param.20) | copy-start | bytes 9220
  259.9 6.6 %copy-start.5 = (f32[768]{0:T(1024)S(1)}, f32[768]{0:T(1024)}, u32[]{:S(2)}) copy-start(f32[768]{0:T(1024)} %param.21) | copy-start | bytes 9220
  259.9 37.9 %all-to-all-start.3 = ((bf16[4,512,384]{2,1,0:T(8,128)(2,1)}), bf16[4,512,384]{2,1,0:T(8,128)(2,1)S(1)}, u32[]{:S(2)}, u32[]{:S(2)}) async-start(bf16[4,512,384]{2,1,0:T(8,128)(2,1)} %shard_map.130), calls=%async_computation.3 | async-start | bytes 3145728 | tf_op jit(solution)/shard_map/all_to_all | solution.py:231
  297.9 1.2 copy-start.1

commit v3 on v2

v3 whole, which is shorter than its diff:
```python
import functools
import math

import jax
import jax.numpy as jnp
from jax import lax
from jax.experimental import pallas as pl
from jax.experimental.pallas import tpu as pltpu
from jax.sharding import PartitionSpec as P

HDIM = 64
BLOCK = 64
MAXK = 8
CAP = 16
PAIR = 2 * HDIM
MESH = pl.DeviceIdType.MESH
VMEM_LIMIT = 56 * 1024 * 1024


def vmem(count):
    return [pl.BlockSpec(memory_space=pltpu.VMEM)] * count


def smem(count):
    return [pl.BlockSpec(memory_space=pltpu.SMEM)] * count


def params():
    return pltpu.CompilerParams(vmem_limit_bytes=VMEM_LIMIT)


def normed(values, gain):
    center = values - jnp.mean(values, axis=-1, keepdims=True)
    spread = jnp.mean(center * center, axis=-1, keepdims=True)
    return center * lax.rsqrt(spread + 1e-05) * gain


def dot(a, b):
    return jnp.dot(a, b, preferred_element_type=jnp.float32)


def project_kv_kernel(head_groups, f_ref, wk_ref, wv_ref, *outs):
    rows = f_ref.shape[0]
    tile = min(rows, 256)
    for start in range(0, rows, tile):
        part = f_ref[start : start + tile, :]
        keys = dot(part, wk_ref[...]).astype(jnp.bfloat16)
        values = dot(part, wv_ref[...]).astype(jnp.bfloat16)
        for group in range(head_groups):
            for place, out in enumerate(outs):
                head = group * len(outs) + place
                cols = slice(head * HDIM, (head + 1) * HDIM)
                both = jnp.concatenate([keys[:, cols], values[:, cols]], axis=1)
                out[group, start : start + tile, :] = both


def project_q_kernel(head_groups, node_parts, f_ref, wq_ref, out):
    rows = f_ref.shape[0]
    half = rows // node_parts // 2
    group_cols = wq_ref.shape[1] // head_groups
    for part in range(node_parts):
        low = part * 2 * half
        first = dot(f_ref[low : low + half, :], wq_ref[...]) * (1.0 / math.sqrt(HDIM))
        second = dot(f_ref[low + half : low + 2 * half, :], wq_ref[...]) * (1.0 / math.sqrt(HDIM))
        first, second = first.astype(jnp.bfloat16), second.astype(jnp.bfloat16)
        for group in range(head_groups):
            cols = slice(group * group_cols, (group + 1) * group_cols)
            out[part * head_groups + group] = jnp.concatenate([first[:, cols], second[:, cols]], axis=1)


def exchange_kernel(head_groups, heads, list_ref, slot_ref, count_ref, q_ref, *rest):
    made, out_ref, rest = rest[:heads], rest[heads], rest[heads + 1 :]
    owns, stages, fars = rest[:heads], rest[heads : 2 * heads], rest[2 * heads : 3 * heads]
    queries, attended, back, kv_send, kv_recv, far_send, far_recv, row_send, row_recv = rest[3 * heads :]
    head_devs, half, _ = q_ref.shape
    node_devs = list_ref.shape[0] // CAP
    device_blocks = made[0].shape[1]
    half_blocks = half // BLOCK
    node_parts = head_devs // head_groups
    node, me = lax.axis_index("node"), lax.axis_index("head")
    part = me // head_groups
    head_peers = [lax.rem(me + k, head_devs) for k in range(1, head_devs)]
    node_peers = [lax.rem(node + k, node_devs) for k in range(1, node_devs)]

    barrier = pltpu.get_barrier_semaphore()
    for peer in head_peers:
        pl.semaphore_signal(barrier, inc=1, device_id=(node, peer), device_id_type=MESH)
    for peer in node_peers:
        pl.semaphore_signal(barrier, inc=1, device_id=(peer, me), device_id_type=MESH)
    pl.semaphore_wait(barrier, len(head_peers) + len(node_peers))

    def remote(source, target, send, recv, device):
        return pltpu.make_async_remote_copy(
            src_ref=source, dst_ref=target, send_sem=send, recv_sem=recv, device_id=device, device_id_type=MESH
        )

    here = pl.ds(me * device_blocks, device_blocks)
    kv_copies = [
        [
            remote(
                made[h].at[lax.rem(peer, head_groups)],
                owns[h].at[here],
                kv_send.at[h, k],
                kv_recv.at[h, k],
                (node, peer),
            )
            for k, peer in enumerate(head_peers)
        ]
        for h in range(heads)
    ]
    q_copies = [
        remote(q_ref.at[peer], queries.at[me], row_send.at[0, k], row_recv.at[0, k], (node, peer))
        for k, peer in enumerate(head_peers)
    ]
    mine = pl.ds(node * CAP, CAP)
    far_copies = [
        [
            remote(
                stages[h].at[pl.ds(peer * CAP, CAP)],
                fars[h].at[mine],
                far_send.at[h, k],
                far_recv.at[h, k],
                (peer, me),
            )
            for k, peer in enumerate(node_peers)
        ]
        for h in range(heads)
    ]
    back_copies = [
        remote(attended.at[peer], back.at[me], row_send.at[1, k], row_recv.at[1, k], (node, peer))
        for k, peer in enumerate(head_peers)
    ]

    for copy in kv_copies[0]:
        copy.start()
    queries[me] = q_ref[me]
    for h in range(heads):
        owns[h][here] = made[h][lax.rem(me, head_groups)]
    for h in range(heads):
        for copy in kv_copies[h]:
            copy.wait_send()
        for copy in kv_copies[h + 1] if h + 1 < heads else q_copies:
            copy.start()
        for copy in kv_copies[h]:
            copy.wait_recv()

        def pick(i, step, h=h):
            stages[h][i] = owns[h][list_ref[i]]
            return step

        lax.fori_loop(0, node_devs * CAP, pick, 0, unroll=4)
        for copy in far_copies[h]:
            copy.start()
        fars[h][mine] = stages[h][mine]
    for copy in q_copies:
        copy.wait()

    column = lax.broadcasted_iota(jnp.int32, (1, (MAXK + 1) * BLOCK), 1)
    low = lax.broadcasted_iota(jnp.int32, (1, PAIR), 1) < HDIM

    def attend(h, source, i):
        row = pl.multiple_of(i * BLOCK, BLOCK)
        for side in range(2):
            block = (source * node_parts + part) * (2 * half_blocks) + side * half_blocks + i
            unit = side * heads + h
            pair = queries[source, pl.ds(row, BLOCK), unit // 2 * PAIR : (unit // 2 + 1) * PAIR]
            if unit % 2:
                pair = jnp.concatenate([pair[:, HDIM:], pair[:, :HDIM]], axis=1)
            query = jnp.where(low, pair, jnp.zeros_like(pair))
            both = jnp.concatenate(
                [owns[h][block]] + [fars[h][slot_ref[block * MAXK + j]] for j in range(MAXK)], axis=0
            )
            scores = lax.dot_general(query, both, (((1,), (1,)), ((), ())), preferred_element_type=jnp.float32)
            scores = jnp.where(column < (count_ref[block] + 1) * BLOCK, scores, -1e30)
            weights = jnp.exp(scores - jnp.max(scores, axis=-1, keepdims=True))
            total = jnp.sum(weights, axis=-1, keepdims=True)
            result = (dot(weights.astype(jnp.bfloat16), both) / total).astype(jnp.bfloat16)
            attended[source, pl.ds(row, BLOCK), unit * HDIM : (unit + 1) * HDIM] = result[:, HDIM:]

    def attend_source(h, source):
        def one(i, step):
            attend(h, source, 2 * i)
            attend(h, source, 2 * i + 1)
            return step

        lax.fori_loop(0, half_blocks // 2, one, 0)

    for h in range(heads):
        for copy in far_copies[h]:
            copy.wait()
        if h + 1 < heads:

            def every(source, step, h=h):
                attend_source(h, source)
                return step

            lax.fori_loop(0, head_devs, every, 0)
    for copy, peer in zip(back_copies, head_peers):
        attend_source(heads - 1, peer)
        copy.start()
    attend_source(heads - 1, me)
    back[me] = attended[me]
    for copy in back_copies:
        copy.wait()
    out_ref[...] = back[...]


def finish_kernel(head_groups, f_ref, b_ref, wo_ref, wu_ref, wd_ref, ga_ref, gf_ref, out_ref):
    devices, half, width = b_ref.shape
    cols = width // 2
    tile = min(half, 256)
    for part in range(devices // head_groups):
        for side in range(2):
            for start in range(0, half, tile):
                low = (part * 2 + side) * half + start
                attended = jnp.concatenate(
                    [
                        b_ref[part * head_groups + group, start : start + tile, side * cols : (side + 1) * cols]
                        for group in range(head_groups)
                    ],
                    axis=1,
                )
                mixed = f_ref[low : low + tile, :].astype(jnp.float32) + dot(attended, wo_ref[...])
                first = normed(mixed, ga_ref[...]).astype(jnp.bfloat16)
                hidden = jnp.maximum(dot(first, wu_ref[...]), 0.0).astype(jnp.bfloat16)
                total = first.astype(jnp.float32) + dot(hidden, wd_ref[...])
                out_ref[low : low + tile, :] = normed(total, gf_ref[...]).astype(jnp.bfloat16)


def per_device(
    features,
    w_query,
    w_key,
    w_value,
    w_out,
    w_up,
    w_down,
    gain_attn,
    gain_ffn,
    send_list,
    edge_owner,
    edge_slot,
    edge_count,
):
    head_devs = lax.axis_size("head")
    head_index = lax.axis_index("head")
    local_rows, width = features.shape
    head_groups = math.gcd(width // HDIM, head_devs)
    node_parts = head_devs // head_groups
    part_index = head_index // head_groups
    head_cols = width // head_groups
    half = local_rows // node_parts // 2
    bf16 = jnp.bfloat16
    group_blocks = head_devs * local_rows // BLOCK
    heads = head_cols // HDIM
    listed = send_list.reshape(-1)
    peers = head_devs - 1
    node_peers = lax.axis_size("node") - 1

    kvs = pl.pallas_call(
        functools.partial(project_kv_kernel, head_groups),
        out_shape=[jax.ShapeDtypeStruct((head_groups, local_rows, PAIR), bf16)] * heads,
        in_specs=vmem(3),
        out_specs=vmem(heads),
        compiler_params=params(),
    )(features, w_key, w_value)
    queries = pl.pallas_call(
        functools.partial(project_q_kernel, head_groups, node_parts),
        out_shape=jax.ShapeDtypeStruct((head_devs, half, 2 * head_cols), bf16),
        in_specs=vmem(2),
        out_specs=vmem(1)[0],
        compiler_params=params(),
        cost_estimate=pl.CostEstimate(
            flops=2 * local_rows * width * width, bytes_accessed=6 * local_rows * width, transcendentals=0
        ),
    )(features, w_query)

    slots = (edge_owner * CAP + edge_slot).reshape(-1)
    rows_shape = (head_devs, half, 2 * head_cols)
    back = pl.pallas_call(
        functools.partial(exchange_kernel, head_groups, heads),
        out_shape=jax.ShapeDtypeStruct(rows_shape, bf16),
        in_specs=smem(3) + vmem(1 + heads),
        out_specs=vmem(1)[0],
        scratch_shapes=[pltpu.VMEM((group_blocks, BLOCK, PAIR), bf16)] * heads
        + [pltpu.VMEM((listed.shape[0], BLOCK, PAIR), bf16)] * (2 * heads)
        + [pltpu.VMEM(rows_shape, bf16)] * 3
        + [pltpu.SemaphoreType.DMA((heads, peers))] * 2
        + [pltpu.SemaphoreType.DMA((heads, node_peers))] * 2
        + [pltpu.SemaphoreType.DMA((2, peers))] * 2,
        compiler_params=pltpu.CompilerParams(
            vmem_limit_bytes=VMEM_LIMIT, collective_id=0, has_side_effects=True
        ),
    )(
        listed,
        slots,
        edge_count,
        queries,
        *[kv.reshape(head_groups, local_rows // BLOCK, BLOCK, PAIR) for kv in kvs],
    )

    return pl.pallas_call(
        functools.partial(finish_kernel, head_groups),
        out_shape=jax.ShapeDtypeStruct((local_rows, width), bf16),
        in_specs=vmem(7),
        out_specs=vmem(1)[0],
        compiler_params=params(),
    )(features, back, w_out, w_up, w_down, gain_attn.reshape(1, -1), gain_ffn.reshape(1, -1))


def solution(mesh):
    return jax.shard_map(
        per_device,
        mesh=mesh,
        in_specs=(
            P(("node", "head"), None),
            P(),
            P(),
            P(),
            P(),
            P(),
            P(),
            P(),
            P(),
            P("node", None, None),
            P("node", None),
            P("node", None),
            P("node"),
        ),
        out_specs=P(("node", "head"), None),
        check_vma=False,
    )
```

time: 317 us -> 219 us (0.69)
  waiting for transfers between devices: 194 us -> 0 us
  Pallas kernels: 92.5 us -> 215 us
  starting transfers between devices: 22.6 us -> 0 us
    all_to_all x4 -> x0, waiting for transfers between devices: 194 us -> none  [the longest x1 70.8 us: per_device(): lax.all_to_all(outgoing, 'node', split_axis=0, concat_axis=0, tiled=True)]
    pallas_call x3 -> x2, Pallas kernels: 74.6 us -> 197 us  [the longest x1 190 us: per_device(): pl.pallas_call(functools.partial(exchange_kernel, head_groups, heads), ou...]
    all_to_all x4 -> x0, starting transfers between devices: 22.6 us -> none  [the longest x1 6.68 us: per_device(): lax.all_to_all(queries, 'head', split_axis=0, concat_axis=0, tiled=True)]
  transfers between devices with their start and end apart: 4 -> 0, of which waited for: 4 -> 0; matrix products, arithmetic and copies ran while one was open for 1% -> 0% of each run, Pallas kernels for 3% -> 0%
where the time goes in v3:
time: 219 us; the launch traced here: 217 us
  Pallas kernels  215 us (98%)
  local copies, waits for them, and re-layouts  2.6 us (1%)
    pallas_call x1, Pallas kernels, per_device(): pl.pallas_call(functools.partial(exchange_kernel, head_groups, heads), ou...  190 us
    pallas_call x1, Pallas kernels, per_device(): pl.pallas_call(functools.partial(finish_kernel, head_groups), out_shape=j...  13.5 us
    pallas_call x1, Pallas kernels, per_device(): pl.pallas_call(functools.partial(project_kv_kernel, head_groups), out_sha...  6.46 us
    pallas_call x1, Pallas kernels, per_device(): pl.pallas_call(functools.partial(project_q_kernel, head_groups, node_part...  4.39 us

profile of v3, /device:TPU:24, one launch (start us, length us, event | category | flops | bytes accessed | tf_op | source)
XLA Modules:
  0.0 217.2 jit_solution(7687445396539978973)
XLA Ops:
  0.0 6.5 %shard_map.128 = (bf16[4,1024,128]{2,1,0:T(8,128)(2,1)}, bf16[4,1024,128]{2,1,0:T(8,128)(2,1)}, bf16[4,1024,128]{2,1,0:T(8,128)(2,1)}) custom-call(bf16[1024,768]{1,0:T(8,128)(2,1)} %f_ref.5, bf16[768,768]{1,0:T(8,128)(2,1)} %wk_ref.1, bf16[768,768]{1,0:T(8,128)(2,1)} %wv_ref.1), custom_call_target="tpu_custom_call" | custom-call | tf_op jit(solution)/shard_map/pallas_call | solution.py:260
  6.5 0.0 copy-start
  6.5 0.0 copy-start.1
  6.5 0.0 copy-start.4
  6.5 4.4 %shard_map.127.q_ref = bf16[4,512,384]{2,1,0:T(8,128)(2,1)} custom-call(bf16[1024,768]{1,0:T(8,128)(2,1)} %f_ref.5, bf16[768,768]{1,0:T(8,128)(2,1)} %wq_ref.1), custom_call_target="tpu_custom_call" | custom-call | flops 1207959552 | bytes 4718592 | tf_op jit(solution)/shard_map/pallas_call | solution.py:267
  10.9 0.0 copy-done
  10.9 0.0 copy-done.1
  10.9 0.1 copy.14
  11.0 0.7 reshape.22.slot_ref
  11.6 0.0 copy-done.4
  11.6 0.7 reshape.21.list_ref
  12.3 0.0 copy-start.2
  12.3 0.0 copy-start.3
  12.3 190.2 %shard_map.129.b_ref = bf16[4,512,384]{2,1,0:T(8,128)(2,1)} custom-call(s32[128]{0:T(128)} %reshape.21.list_ref, s32[512]{0:T(512)} %reshape.22.slot_ref, s32[64]{0:T(128)} %count_ref.1, bf16[4,512,384]{2,1,0:T(8,128)(2,1)} %shard_map.127.q_ref, bf16[4,16,64,128]{3,2,1,0:T(8,128)(2,1)} %bitcast.3, bf16[4,16,64,128]{3,2,1,0:T(8,128)(2,1)} %bitcast.4, ...), custom_call_target="tpu_custom_call" | custom-call | tf_op jit(solution)/shard_map/pallas_call | solution.py:280
  202.5 0.0 copy-done.2
  202.5 0.6 reshape.26.ga_ref
  203.1 0.0 copy-done.3
  203.1 0.6 reshape.27.gf_ref
  203.7 13.5 %shard_map.130 = bf16[1024,768]{1,0:T(8,128)(2,1)} custom-call(bf16[1024,768]{1,0:T(8,128)(2,1)} %f_ref.5, bf16[4,512,384]{2,1,0:T(8,128)(2,1)} %shard_map.129.b_ref, bf16[768,768]{1,0:T(8,128)(2,1)} %wo_ref.1, bf16[768,1536]{1,0:T(8,128)(2,1)} %wu_ref.1, bf16[1536,768]{1,0:T(8,128)(2,1)} %wd_ref.1, f32[1,768]{1,0:T(1,128)} %reshape.26.ga_ref, ...), custom_call_target="tpu_custom_call" | custom-call | tf_op jit(solution)/shard_map/pallas_call | solution.py:302
  (1 shorter events, 0.0 us)
Async XLA Ops:
  6.5 4.4 %copy-start = (s32[64,8]{0,1:T(8,128)S(1)}, s32[64,8]{0,1:T(8,128)}, u32[]{:S(2)}) copy-start(s32[64,8]{0,1:T(8,128)} %param.24) | copy-start | bytes 6148
  6.5 4.4 %copy-start.1 = (s32[64,8]{0,1:T(8,128)S(1)}, s32[64,8]{0,1:T(8,128)}, u32[]{:S(2)}) copy-start(s32[64,8]{0,1:T(8,128)} %param.23) | copy-start | bytes 6148
  6.5 5.1 %copy-start.4 = (s32[1,8,16]{2,1,0:T(8,128)S(1)}, s32[1,8,16]{2,1,0:T(8,128)}, u32[]{:S(2)}) copy-start(s32[1,8,16]{2,1,0:T(8,128)} %param.22) | copy-start | bytes 1540
  12.3 190.2 %copy-start.2 = (f32[768]{0:T(1024)S(1)}, f32[768]{0:T(1024)}, u32[]{:S(2)}) copy-start(f32[768]{0:T(1024)} %param.20) | copy-start | bytes 9220
  12.3 190.8 %copy-start.3 = (f32[768]{0:T(1024)S(1)}, f32[768]{0:T(1024)}, u32[]{:S(2)}) copy-start(f32[768]{0:T(1024)} %param.21) | copy-start | bytes 9220

commit v4 on v3

--- a/solution.py
+++ b/solution.py
@@ -54,25 +54,28 @@
                 out[group, start : start + tile, :] = both
 
 
-def project_q_kernel(head_groups, node_parts, f_ref, wq_ref, out):
+def project_q_kernel(head_groups, node_parts, f_ref, wq_ref, *outs):
     rows = f_ref.shape[0]
     half = rows // node_parts // 2
-    group_cols = wq_ref.shape[1] // head_groups
     for part in range(node_parts):
         low = part * 2 * half
         first = dot(f_ref[low : low + half, :], wq_ref[...]) * (1.0 / math.sqrt(HDIM))
         second = dot(f_ref[low + half : low + 2 * half, :], wq_ref[...]) * (1.0 / math.sqrt(HDIM))
         first, second = first.astype(jnp.bfloat16), second.astype(jnp.bfloat16)
         for group in range(head_groups):
-            cols = slice(group * group_cols, (group + 1) * group_cols)
-            out[part * head_groups + group] = jnp.concatenate([first[:, cols], second[:, cols]], axis=1)
-
-
-def exchange_kernel(head_groups, heads, list_ref, slot_ref, count_ref, q_ref, *rest):
-    made, out_ref, rest = rest[:heads], rest[heads], rest[heads + 1 :]
+            for place, out in enumerate(outs):
+                head = group * len(outs) + place
+                cols = slice(head * HDIM, (head + 1) * HDIM)
+                out[part * head_groups + group] = jnp.concatenate([first[:, cols], second[:, cols]], axis=1)
+
+
+def exchange_kernel(head_groups, heads, list_ref, slot_ref, count_ref, *rest):
+    q_refs, made, outs, rest = rest[:heads], rest[heads : 2 * heads], rest[2 * heads : 3 * heads], rest[3 * heads :]
     owns, stages, fars = rest[:heads], rest[heads : 2 * heads], rest[2 * heads : 3 * heads]
-    queries, attended, back, kv_send, kv_recv, far_send, far_recv, row_send, row_recv = rest[3 * heads :]
-    head_devs, half, _ = q_ref.shape
+    rest = rest[3 * heads :]
+    queries, attended, backs = rest[:heads], rest[heads : 2 * heads], rest[2 * heads : 3 * heads]
+    kv_send, kv_recv, far_send, far_recv, row_send, row_recv = rest[3 * heads :]
+    head_devs, half, _ = q_refs[0].shape
     node_devs = list_ref.shape[0] // CAP
     device_blocks = made[0].shape[1]
     half_blocks = half // BLOCK
@@ -109,8 +112,11 @@
         for h in range(heads)
     ]
     q_copies = [
-        remote(q_ref.at[peer], queries.at[me], row_send.at[0, k], row_recv.at[0, k], (node, peer))
-        for k, peer in enumerate(head_peers)
+        [
+            remote(q_refs[h].at[peer], queries[h].at[me], row_send.at[h, k], row_recv.at[h, k], (node, peer))
+            for k, peer in enumerate(head_peers)
+        ]
+        for h in range(heads)
     ]
     mine = pl.ds(node * CAP, CAP)
     far_copies = [
@@ -127,33 +133,47 @@
         for h in range(heads)
     ]
     back_copies = [
-        remote(attended.at[peer], back.at[me], row_send.at[1, k], row_recv.at[1, k], (node, peer))
-        for k, peer in enumerate(head_peers)
+        [
+            remote(
+                attended[h].at[peer],
+                backs[h].at[me],
+                row_send.at[heads + h, k],
+                row_recv.at[heads + h, k],
+                (node, peer),
+            )
+            for k, peer in enumerate(head_peers)
+        ]
+        for h in range(heads)
     ]
 
     for copy in kv_copies[0]:
         copy.start()
-    queries[me] = q_ref[me]
     for h in range(heads):
+        queries[h][me] = q_refs[h][me]
         owns[h][here] = made[h][lax.rem(me, head_groups)]
-    for h in range(heads):
-        for copy in kv_copies[h]:
+
+    def start(copies):
+        for copy in copies:
+            copy.start()
+
+    def sent(copies):
+        for copy in copies:
             copy.wait_send()
-        for copy in kv_copies[h + 1] if h + 1 < heads else q_copies:
-            copy.start()
-        for copy in kv_copies[h]:
+
+    def landed(copies):
+        for copy in copies:
             copy.wait_recv()
 
-        def pick(i, step, h=h):
+    def pass_on(h):
+        landed(kv_copies[h])
+
+        def pick(i, step):
             stages[h][i] = owns[h][list_ref[i]]
             return step
 
         lax.fori_loop(0, node_devs * CAP, pick, 0, unroll=4)
-        for copy in far_copies[h]:
-            copy.start()
+        start(far_copies[h])
         fars[h][mine] = stages[h][mine]
-    for copy in q_copies:
-        copy.wait()
 
     column = lax.broadcasted_iota(jnp.int32, (1, (MAXK + 1) * BLOCK), 1)
     low = lax.broadcasted_iota(jnp.int32, (1, PAIR), 1) < HDIM
@@ -162,9 +182,8 @@
         row = pl.multiple_of(i * BLOCK, BLOCK)
         for side in range(2):
             block = (source * node_parts + part) * (2 * half_blocks) + side * half_blocks + i
-            unit = side * heads + h
-            pair = queries[source, pl.ds(row, BLOCK), unit // 2 * PAIR : (unit // 2 + 1) * PAIR]
-            if unit % 2:
+            pair = queries[h][source, pl.ds(row, BLOCK), :]
+            if side:
                 pair = jnp.concatenate([pair[:, HDIM:], pair[:, :HDIM]], axis=1)
             query = jnp.where(low, pair, jnp.zeros_like(pair))
             both = jnp.concatenate(
@@ -175,7 +194,7 @@
             weights = jnp.exp(scores - jnp.max(scores, axis=-1, keepdims=True))
             total = jnp.sum(weights, axis=-1, keepdims=True)
             result = (dot(weights.astype(jnp.bfloat16), both) / total).astype(jnp.bfloat16)
-            attended[source, pl.ds(row, BLOCK), unit * HDIM : (unit + 1) * HDIM] = result[:, HDIM:]
+            attended[h][source, pl.ds(row, BLOCK), side * HDIM : (side + 1) * HDIM] = result[:, HDIM:]
 
     def attend_source(h, source):
         def one(i, step):
@@ -185,29 +204,51 @@
 
         lax.fori_loop(0, half_blocks // 2, one, 0)
 
-    for h in range(heads):
-        for copy in far_copies[h]:
-            copy.wait()
+    def attend_head(h):
+        landed(q_copies[h])
+        landed(far_copies[h])
         if h + 1 < heads:
 
-            def every(source, step, h=h):
+            def every(source, step):
                 attend_source(h, source)
                 return step
 
             lax.fori_loop(0, head_devs, every, 0)
-    for copy, peer in zip(back_copies, head_peers):
-        attend_source(heads - 1, peer)
-        copy.start()
-    attend_source(heads - 1, me)
-    back[me] = attended[me]
-    for copy in back_copies:
-        copy.wait()
-    out_ref[...] = back[...]
-
-
-def finish_kernel(head_groups, f_ref, b_ref, wo_ref, wu_ref, wd_ref, ga_ref, gf_ref, out_ref):
-    devices, half, width = b_ref.shape
-    cols = width // 2
+            start(back_copies[h])
+        else:
+            for copy, peer in zip(back_copies[h], head_peers):
+                attend_source(h, peer)
+                copy.start()
+            attend_source(h, me)
+        backs[h][me] = attended[h][me]
+
+    sent(kv_copies[0])
+    start(q_copies[0])
+    pass_on(0)
+    sent(q_copies[0])
+    for h in range(1, heads):
+        start(kv_copies[h])
+        if h > 1:
+            attend_head(h - 2)
+        sent(kv_copies[h])
+        if h + 1 == heads:
+            for later in range(1, heads):
+                start(q_copies[later])
+        pass_on(h)
+    for h in range(max(heads - 2, 0), heads):
+        attend_head(h)
+    for h in range(heads):
+        if h:
+            sent(q_copies[h])
+        sent(far_copies[h])
+        sent(back_copies[h])
+        landed(back_copies[h])
+        outs[h][...] = backs[h][...]
+
+
+def finish_kernel(head_groups, heads, f_ref, *rest):
+    b_refs, (wo_ref, wu_ref, wd_ref, ga_ref, gf_ref, out_ref) = rest[:heads], rest[heads:]
+    devices, half, _ = b_refs[0].shape
     tile = min(half, 256)
     for part in range(devices // head_groups):
         for side in range(2):
@@ -215,8 +256,9 @@
                 low = (part * 2 + side) * half + start
                 attended = jnp.concatenate(
                     [
-                        b_ref[part * head_groups + group, start : start + tile, side * cols : (side + 1) * cols]
+                        b_ref[part * head_groups + group, start : start + tile, side * HDIM : (side + 1) * HDIM]
                         for group in range(head_groups)
+                        for b_ref in b_refs
                     ],
                     axis=1,
                 )
@@ -266,9 +308,9 @@
     )(features, w_key, w_value)
     queries = pl.pallas_call(
         functools.partial(project_q_kernel, head_groups, node_parts),
-        out_shape=jax.ShapeDtypeStruct((head_devs, half, 2 * head_cols), bf16),
+        out_shape=[jax.ShapeDtypeStruct((head_devs, half, PAIR), bf16)] * heads,
         in_specs=vmem(2),
-        out_specs=vmem(1)[0],
+        out_specs=vmem(heads),
         compiler_params=params(),
         cost_estimate=pl.CostEstimate(
             flops=2 * local_rows * width * width, bytes_accessed=6 * local_rows * width, transcendentals=0
@@ -276,18 +318,18 @@
     )(features, w_query)
 
     slots = (edge_owner * CAP + edge_slot).reshape(-1)
-    rows_shape = (head_devs, half, 2 * head_cols)
-    back = pl.pallas_call(
+    rows_shape = (head_devs, half, PAIR)
+    backs = pl.pallas_call(
         functools.partial(exchange_kernel, head_groups, heads),
-        out_shape=jax.ShapeDtypeStruct(rows_shape, bf16),
-        in_specs=smem(3) + vmem(1 + heads),
-        out_specs=vmem(1)[0],
+        out_shape=[jax.ShapeDtypeStruct(rows_shape, bf16)] * heads,
+        in_specs=smem(3) + vmem(2 * heads),
+        out_specs=vmem(heads),
         scratch_shapes=[pltpu.VMEM((group_blocks, BLOCK, PAIR), bf16)] * heads
         + [pltpu.VMEM((listed.shape[0], BLOCK, PAIR), bf16)] * (2 * heads)
-        + [pltpu.VMEM(rows_shape, bf16)] * 3
+        + [pltpu.VMEM(rows_shape, bf16)] * (3 * heads)
         + [pltpu.SemaphoreType.DMA((heads, peers))] * 2
         + [pltpu.SemaphoreType.DMA((heads, node_peers))] * 2
-        + [pltpu.SemaphoreType.DMA((2, peers))] * 2,
+        + [pltpu.SemaphoreType.DMA((2 * heads, peers))] * 2,
         compiler_params=pltpu.CompilerParams(
             vmem_limit_bytes=VMEM_LIMIT, collective_id=0, has_side_effects=True
         ),
@@ -295,17 +337,17 @@
         listed,
         slots,
         edge_count,
-        queries,
+        *queries,
         *[kv.reshape(head_groups, local_rows // BLOCK, BLOCK, PAIR) for kv in kvs],
     )
 
     return pl.pallas_call(
-        functools.partial(finish_kernel, head_groups),
+        functools.partial(finish_kernel, head_groups, heads),
         out_shape=jax.ShapeDtypeStruct((local_rows, width), bf16),
-        in_specs=vmem(7),
+        in_specs=vmem(6 + heads),
         out_specs=vmem(1)[0],
         compiler_params=params(),
-    )(features, back, w_out, w_up, w_down, gain_attn.reshape(1, -1), gain_ffn.reshape(1, -1))
+    )(features, *backs, w_out, w_up, w_down, gain_attn.reshape(1, -1), gain_ffn.reshape(1, -1))
 
 
 def solution(mesh):

time: 219 us -> 186 us (0.85)
  Pallas kernels: 215 us -> 183 us
    pallas_call x1, Pallas kernels: 190 us -> 159 us  [per_device(): pl.pallas_call(functools.partial(exchange_kernel, head_groups, heads), ou...]
where the time goes in v4:
time: 186 us
  Pallas kernels  183 us (98%)
  local copies, waits for them, and re-layouts  2.65 us (1%)
    pallas_call x1, Pallas kernels, per_device(): pl.pallas_call(functools.partial(exchange_kernel, head_groups, heads), ou...  159 us
    pallas_call x1, Pallas kernels, per_device(): pl.pallas_call(functools.partial(finish_kernel, head_groups, heads), out_...  13.5 us
    pallas_call x1, Pallas kernels, per_device(): pl.pallas_call(functools.partial(project_kv_kernel, head_groups), out_sha...  6.5 us
    pallas_call x1, Pallas kernels, per_device(): pl.pallas_call(functools.partial(project_q_kernel, head_groups, node_part...  4.41 us

profile of v4, /device:TPU:24, one launch (start us, length us, event | category | flops | bytes accessed | tf_op | source)
XLA Modules:
  0.0 186.0 jit_solution(8428590564058848086)
XLA Ops:
  0.0 6.5 %shard_map.128 = (bf16[4,1024,128]{2,1,0:T(8,128)(2,1)}, bf16[4,1024,128]{2,1,0:T(8,128)(2,1)}, bf16[4,1024,128]{2,1,0:T(8,128)(2,1)}) custom-call(bf16[1024,768]{1,0:T(8,128)(2,1)} %f_ref.5, bf16[768,768]{1,0:T(8,128)(2,1)} %wk_ref.1, bf16[768,768]{1,0:T(8,128)(2,1)} %wv_ref.1), custom_call_target="tpu_custom_call" | custom-call | tf_op jit(solution)/shard_map/pallas_call | solution.py:302
  6.5 0.0 copy-start
  6.5 0.0 copy-start.1
  6.5 0.0 copy-start.4
  6.5 4.4 %shard_map.127 = (bf16[4,512,128]{2,1,0:T(8,128)(2,1)}, bf16[4,512,128]{2,1,0:T(8,128)(2,1)}, bf16[4,512,128]{2,1,0:T(8,128)(2,1)}) custom-call(bf16[1024,768]{1,0:T(8,128)(2,1)} %f_ref.5, bf16[768,768]{1,0:T(8,128)(2,1)} %wq_ref.1), custom_call_target="tpu_custom_call" | custom-call | flops 1207959552 | bytes 4718592 | tf_op jit(solution)/shard_map/pallas_call | solution.py:309
  10.9 0.0 copy-done
  10.9 0.0 copy-done.1
  10.9 0.1 copy.14
  11.0 0.7 reshape.22.slot_ref
  11.7 0.0 copy-done.4
  11.7 0.7 reshape.21.list_ref
  12.4 0.0 copy-start.2
  12.4 0.0 copy-start.3
  12.4 158.9 %shard_map.129 = (bf16[4,512,128]{2,1,0:T(8,128)(2,1)}, bf16[4,512,128]{2,1,0:T(8,128)(2,1)}, bf16[4,512,128]{2,1,0:T(8,128)(2,1)}) custom-call(s32[128]{0:T(128)} %reshape.21.list_ref, s32[512]{0:T(512)} %reshape.22.slot_ref, s32[64]{0:T(128)} %count_ref.1, bf16[4,512,128]{2,1,0:T(8,128)(2,1)} %get-tuple-element.14.rest_0_, ...), custom_call_target="tpu_custom_call" | custom-call | tf_op jit(solution)/shard_map/pallas_call | solution.py:322
  171.3 0.0 copy-done.2
  171.3 0.6 reshape.26.rest_6_
  171.9 0.0 copy-done.3
  171.9 0.6 reshape.27.rest_7_
  172.5 13.5 %shard_map.130 = bf16[1024,768]{1,0:T(8,128)(2,1)} custom-call(bf16[1024,768]{1,0:T(8,128)(2,1)} %f_ref.5, bf16[4,512,128]{2,1,0:T(8,128)(2,1)} %get-tuple-element.20.rest_0_, bf16[4,512,128]{2,1,0:T(8,128)(2,1)} %get-tuple-element.21.rest_1_, bf16[4,512,128]{2,1,0:T(8,128)(2,1)} %get-tuple-element.22.rest_2_, bf16[768,768]{1,0:T(8,128)(2,1)} %rest_3_.1, ...), custom_call_target="tpu_custom_call" | custom-call | tf_op jit(solution)/shard_map/pallas_call | solution.py:344
  (1 shorter events, 0.0 us)
Async XLA Ops:
  6.5 4.4 %copy-start = (s32[64,8]{0,1:T(8,128)S(1)}, s32[64,8]{0,1:T(8,128)}, u32[]{:S(2)}) copy-start(s32[64,8]{0,1:T(8,128)} %param.24) | copy-start | bytes 6148
  6.5 4.4 %copy-start.1 = (s32[64,8]{0,1:T(8,128)S(1)}, s32[64,8]{0,1:T(8,128)}, u32[]{:S(2)}) copy-start(s32[64,8]{0,1:T(8,128)} %param.23) | copy-start | bytes 6148
  6.5 5.2 %copy-start.4 = (s32[1,8,16]{2,1,0:T(8,128)S(1)}, s32[1,8,16]{2,1,0:T(8,128)}, u32[]{:S(2)}) copy-start(s32[1,8,16]{2,1,0:T(8,128)} %param.22) | copy-start | bytes 1540
  12.4 158.9 %copy-start.2 = (f32[768]{0:T(1024)S(1)}, f32[768]{0:T(1024)}, u32[]{:S(2)}) copy-start(f32[768]{0:T(1024)} %param.20) | copy-start | bytes 9220
  12.4 159.5 %copy-start.3 = (f32[768]{0:T(1024)S(1)}, f32[768]{0:T(1024)}, u32[]{:S(2)}) copy-start(f32[768]{0:T(1024)} %param.21) | copy-start | bytes 9220
